TPU v7x, 128 devices: a whole 4x4x4 slice. The times are simulated.
128 devices in a mesh: bx: 8 (over y, core), by: 16 (over x, z).
Axes of the slice: x: 4, y: 4, z: 4, core: 2. Of those that a mesh axis runs over, the one named last changes fastest.
Arguments:
- h_old: float32 [20, 512, 2048], P(None, 'bx', 'by'), may hold values from -3 to 0.5
- soil_type: int32 [20, 512, 2048], P(None, 'bx', 'by'), may hold values from 0 to 11
- ks_scale: float32 [20, 512, 2048], P(None, 'bx', 'by'), may hold values from 0.3 to 3
- soil_table: float32 [4, 12], replicated, may hold values from 0.2 to 1
- clump_brick: int32 [1048576], P(('bx', 'by')), may hold values from -1 to 127, as said below
- clump_cell: int32 [1048576], P(('bx', 'by')), may hold values from -1 to 8191, as said below
- root_fraction: float32 [14, 1048576], P(None, ('bx', 'by')), may hold values from 0.05 to 0.3
- transpiration: float32 [1048576], P(('bx', 'by')), may hold values from 0.2 to 2
- infiltration: float32 [1048576], P(('bx', 'by')), may hold values from 0.2 to 2
Outputs:
- pressure: float32 [20, 512, 2048], P(None, 'bx', 'by')
- stress: float32 [1048576], P(('bx', 'by'))
Inputs may be any that keep to these rules, and one draw needn't show every extreme that they name: `clump_brick`: A brick is the 64 x 128 columns with i // 64 and j // 128 fixed, numbered (i // 64) * 16 + j // 128. The slots of one device are the 8192 consecutive entries of its shard; its slots b * 64 to (b + 1) * 64 - 1 hold columns of brick b or are empty, and there the entry is b; -1 marks an empty slot (exactly where clump_cell is -1). `clump_cell`: A slot's entry is the position (i % 64) * 128 + j % 128 of its column within its brick, or -1 when empty; no column is held twice. In every draw one brick has all its columns held, all 64 of its slots filled on every device.
All inputs are finite; a program needn't handle non-finite values.
Results may differ from a plain program's by a relative error of at most 0.000068.
Values sent between devices are 32-bit elements; how exact they have to be, the bound alone decides.
A program may use at most 64 MiB of HBM per device.

v0:
```python
import functools

import jax
import jax.numpy as jnp
from jax import lax
from jax.experimental import pallas as pl
from jax.experimental.pallas import tpu as pltpu
from jax.sharding import PartitionSpec as P

MESH = pl.DeviceIdType.MESH
NX, NY = 8, 16
PEERS = NX * NY
LAY, ROOT = 20, 14
RX, RY = 64, 128
SLOTS = RX * RY
FIELDS = ROOT + 1
BLOCK = 16
TINY = 1e-30
F32, BF16, I32 = jnp.float32, jnp.bfloat16, jnp.int32


def closures(head, alpha, shape_n, exponent, ks, width):
    log_s = shape_n * jnp.log2(alpha * jnp.maximum(-head, TINY))
    log_b = jnp.log2(1.0 + jnp.exp2(log_s))
    log_w = exponent * (log_s - log_b)
    root = jnp.exp2(-0.5 * exponent * log_b)
    inner = 1.0 - jnp.exp2(log_w)
    conduct = ks * root * (inner * inner)
    storage = 0.4 + 2.0 * width * (shape_n - 1.0) * alpha * jnp.exp2(log_w - log_b)
    return root, conduct, storage


def kernel(
    h_hbm, soil_hbm, ks_hbm, table_ref, cell_hbm, root_hbm, transp_hbm, infil_hbm,
    p_out, s_out,
    h, soil, ks_in, cell, root, transp, infil,
    table, fields1, send, recv,
    par_a, par_n, par_e, par_k, par_w,
    pk, sat_old, stor, lat, gsum,
    rinv, low, upp, rhs, val,
    a_mat, b_mat, row_of, acc, grid,
    ypack, yrecv, xrecv, ycomb,
    back, mine,
    in_sem, send_sem, recv_sem, halo_send, halo_recv, ret_send, ret_recv, out_sem,
):
    bx = lax.axis_index("bx")
    by = lax.axis_index("by")
    me = bx * NY + by

    copies = [
        pltpu.make_async_copy(src, dst, in_sem.at[i])
        for i, (src, dst) in enumerate(
            (
                (root_hbm, root), (transp_hbm, transp), (infil_hbm, infil), (cell_hbm, cell),
                (h_hbm, h), (soil_hbm, soil), (ks_hbm, ks_in),
            )
        )
    ]
    for copy in copies:
        copy.start()

    def peer(i):
        dx, dy = i // NY, lax.rem(i, NY)
        return lax.rem(bx + dx, NX), lax.rem(by + dy, NY)

    barrier = pltpu.get_barrier_semaphore()

    def greet(i, carry):
        pl.semaphore_signal(barrier, inc=1, device_id=peer(i), device_id_type=MESH)
        return carry

    lax.fori_loop(1, PEERS, greet, 0)

    lane8 = lax.broadcasted_iota(I32, (8, 128), 1)
    sub8 = lax.broadcasted_iota(I32, (8, 128), 0)
    first_half = lane8 < 64

    for copy in copies[:4]:
        copy.wait()
    fields1[0:6, :] = root[8:14, :]
    fields1[6:7, :] = infil[...]
    fields1[7:8, :] = cell[...].astype(F32)

    def pack(q, carry):
        at = pl.ds(pl.multiple_of(q * 128, 128), 128)
        demand = transp[:, at]
        v0 = root[0:8, at] * demand
        v1 = fields1[:, at] * jnp.where(sub8 < 6, demand, 1.0)
        r0 = pltpu.roll(v0, 64, 1)
        r1 = pltpu.roll(v1, 64, 1)
        send[2 * q] = jnp.where(first_half, v0, r1)
        send[2 * q + 1] = jnp.where(first_half, r0, v1)
        return carry

    lax.fori_loop(0, PEERS // 2, pack, 0)

    pl.semaphore_wait(barrier, PEERS - 1)

    own = pltpu.make_async_copy(send.at[me], recv.at[bx, by], recv_sem.at[bx])
    own.start()

    def push(i, carry):
        tx, ty = peer(i)
        pltpu.make_async_remote_copy(
            send.at[tx * NY + ty], recv.at[bx, by], send_sem, recv_sem.at[bx],
            device_id=(tx, ty), device_id_type=MESH,
        ).start()
        return carry

    lax.fori_loop(1, PEERS, push, 0)

    table[...] = jnp.zeros_like(table)
    table[0:4, 0:12] = table_ref[...]
    for copy in copies[4:]:
        copy.wait()
    t0, t1, t2, t3 = (jnp.broadcast_to(table[i : i + 1, :], (RX, 128)) for i in range(4))
    lane = lax.broadcasted_iota(I32, (RX, 128), 1)

    def first(k, packed):
        kind = soil[k]
        look = lambda t: jnp.take_along_axis(t, kind, axis=1, mode="promise_in_bounds")
        alpha = 4.0 * look(t0)
        shape_n = 1.2 + 2.0 * look(t1)
        ks = 0.75 * look(t2) * ks_in[k]
        width = 0.25 + 0.3 * look(t3)
        exponent = 1.0 - 1.0 / shape_n
        par_a[k], par_n[k], par_e[k], par_k[k], par_w[k] = alpha, shape_n, exponent, ks, width
        head = h[k]
        sq, conduct, storage = closures(head, alpha, shape_n, exponent, ks, width)
        sat_old[k] = sq * sq
        stor[k] = storage
        pk[0, k, 8 : 8 + RX, :] = head
        pk[1, k, 8 : 8 + RX, :] = conduct
        turn = 2 * k + 1
        pair = lane // 2
        packed = jnp.where(pair == k, pltpu.roll(head, turn, 1), packed)
        packed = jnp.where(pair == k + 32, pltpu.roll(conduct, turn + 64, 1), packed)
        return packed

    ypack[0] = lax.fori_loop(0, LAY, first, jnp.zeros((RX, 128), F32))

    def halo_copies(step):
        up = lax.rem(bx + NX - 1, NX), by
        down = lax.rem(bx + 1, NX), by
        left = bx, lax.rem(by + NY - 1, NY)
        right = bx, lax.rem(by + 1, NY)
        moves = (
            (pk.at[:, :, pl.ds(64, 8), :], xrecv.at[step, 0], down),
            (pk.at[:, :, pl.ds(8, 8), :], xrecv.at[step, 1], up),
            (ypack.at[step], yrecv.at[step, 0], right),
            (ypack.at[step], yrecv.at[step, 1], left),
        )
        return [
            pltpu.make_async_remote_copy(
                src, dst, halo_send.at[step, i], halo_recv.at[step, i],
                device_id=to, device_id_type=MESH,
            )
            for i, (src, dst, to) in enumerate(moves)
        ]

    odd = lax.rem(lane, 2) == 1

    def halo_finish(step, moves):
        for move in moves:
            move.wait_recv()
        for move in moves:
            move.wait_send()
        for k in range(LAY):
            pk[0, k, 7:8, :] = xrecv[step, 0, 0, k, 7:8, :]
            pk[0, k, 72:73, :] = xrecv[step, 1, 0, k, 0:1, :]
            pk[1, k, 7:8, :] = jnp.where(bx == 0, -pk[1, k, 8:9, :], xrecv[step, 0, 1, k, 7:8, :])
            pk[1, k, 72:73, :] = jnp.where(
                bx == NX - 1, -pk[1, k, 71:72, :], xrecv[step, 1, 1, k, 0:1, :]
            )
        both = jnp.where(
            odd, pltpu.roll(yrecv[step, 0], 1, 1), pltpu.roll(yrecv[step, 1], 127, 1)
        )
        edge = jnp.logical_or(
            jnp.logical_and(odd, by == 0), jnp.logical_and(jnp.logical_not(odd), by == NY - 1)
        )
        ycomb[...] = jnp.where(edge, -ypack[step], both)

    at_first, at_last = lane == 0, lane == 127

    def sideways(k, carry):
        head, conduct = pk[0, k, 8:72, :], pk[1, k, 8:72, :]
        comb = ycomb[...]
        hp = pltpu.roll(comb, 127 - 2 * k, 1)
        hk = pltpu.roll(comb, 63 - 2 * k, 1)
        left_p = jnp.where(at_first, hp, pltpu.roll(head, 1, 1))
        left_k = jnp.where(at_first, hk, pltpu.roll(conduct, 1, 1))
        right_p = jnp.where(at_last, hp, pltpu.roll(head, 127, 1))
        right_k = jnp.where(at_last, hk, pltpu.roll(conduct, 127, 1))
        gl, gr = conduct + left_k, conduct + right_k
        gu, gd = conduct + pk[1, k, 7:71, :], conduct + pk[1, k, 9:73, :]
        gsum[k] = (gl + gr) + (gu + gd)
        lat[k] = (gl * (head - left_p) + gr * (head - right_p)) + (
            gu * (head - pk[0, k, 7:71, :]) + gd * (head - pk[0, k, 9:73, :])
        )
        return carry

    moves = halo_copies(0)
    for move in moves:
        move.start()
    halo_finish(0, moves)
    lax.fori_loop(0, LAY, sideways, 0)

    def factor_first(r, carry):
        rows = pl.ds(pl.multiple_of(r * BLOCK, BLOCK), BLOCK)
        prow = pl.ds(pl.multiple_of(r * BLOCK + 8, 8), BLOCK)
        head, conduct = pk[0, 0, prow, :], pk[1, 0, prow, :]
        v_prev = flux_prev = q_prev = None
        for k in range(LAY):
            target = -lat[k, rows, :]
            diag = stor[k, rows, :] + gsum[k, rows, :]
            if k < LAY - 1:
                head_n, conduct_n = pk[0, k + 1, prow, :], pk[1, k + 1, prow, :]
                v = 2.0 * (conduct + conduct_n)
                flux = v * (head - head_n + 1.0)
                diag = diag + v
                target = target - flux
            else:
                target = target - 4.0 * conduct
            if k > 0:
                target = target + flux_prev
                diag = diag + v_prev - v_prev * q_prev
            inv = 1.0 / diag
            rinv[k, rows, :] = inv
            rhs[k, rows, :] = target * inv
            if k > 0:
                low[k, rows, :] = v_prev * inv
            if k < LAY - 1:
                q_prev = v * inv
                upp[k, rows, :] = q_prev
                head, conduct, v_prev, flux_prev = head_n, conduct_n, v, flux
        return carry

    lax.fori_loop(0, RX // BLOCK, factor_first, 0)

    iota_c = lax.broadcasted_iota(I32, (256, 128), 0)
    iota_r = lax.broadcasted_iota(I32, (32, 128), 0)
    acc[...] = jnp.zeros_like(acc)

    def place(g, carry):
        sx = lax.rem(bx + g, NX)
        pltpu.make_async_copy(recv.at[sx], recv.at[sx], recv_sem.at[sx]).wait()
        for j in range(NY // 2):
            m0, m1 = recv[sx, 2 * j], recv[sx, 2 * j + 1]
            v0 = jnp.where(first_half, m0, pltpu.roll(m1, 64, 1))
            v1 = jnp.where(first_half, pltpu.roll(m0, 64, 1), m1)
            at = slice(j * 128, (j + 1) * 128)
            spot = v1[7:8, :].astype(I32)
            brow = spot >> 7
            col = (spot & 127) + ((brow >> 5) << 7)
            brow = brow & 31
            row_of[sx, :, at] = brow
            b_mat[sx, :, at] = jnp.where(iota_c == col, 1.0, 0.0).astype(BF16)
            hit = iota_r == brow
            h0 = v0.astype(BF16).astype(F32)
            h1 = v1.astype(BF16).astype(F32)
            l0, l1 = v0 - h0, v1 - h1
            for f in range(FIELDS):
                hi = h0[f : f + 1] if f < 8 else h1[f - 8 : f - 7]
                lo = l0[f : f + 1] if f < 8 else l1[f - 8 : f - 7]
                a_mat[f * 64 : f * 64 + 32, at] = jnp.where(hit, hi, 0.0).astype(BF16)
                a_mat[f * 64 + 32 : f * 64 + 64, at] = jnp.where(hit, lo, 0.0).astype(BF16)
        acc[...] += lax.dot_general(
            a_mat[...], b_mat[sx], (((1,), (1,)), ((), ())), preferred_element_type=F32
        )
        return carry

    lax.fori_loop(0, NX, place, 0)
    for f in range(FIELDS):
        both = acc[f * 64 : f * 64 + 32, :] + acc[f * 64 + 32 : f * 64 + 64, :]
        grid[f, 0:32, :] = both[:, :128]
        grid[f, 32:64, :] = both[:, 128:]
    lane_b = lax.broadcasted_iota(I32, (BLOCK, 128), 1)
    pair_b = lane_b // 2

    def solve_first(r, carry):
        rows = pl.ds(pl.multiple_of(r * BLOCK, BLOCK), BLOCK)
        prow = pl.ds(pl.multiple_of(r * BLOCK + 8, 8), BLOCK)
        last = rhs[0, rows, :] + (grid[ROOT, rows, :] - grid[0, rows, :]) * rinv[0, rows, :]
        val[0, rows, :] = last
        for k in range(1, LAY):
            here = rhs[k, rows, :]
            if k < ROOT:
                here = here - grid[k, rows, :] * rinv[k, rows, :]
            last = here + low[k, rows, :] * last
            val[k, rows, :] = last
        packed = jnp.zeros((BLOCK, 128), F32)
        for k in range(LAY - 1, -1, -1):
            if k < LAY - 1:
                last = val[k, rows, :] + upp[k, rows, :] * last
            head = pk[0, k, prow, :] + last
            width = par_w[k, rows, :]
            sq, conduct, storage = closures(
                head, par_a[k, rows, :], par_n[k, rows, :], par_e[k, rows, :],
                par_k[k, rows, :], width,
            )
            pk[0, k, prow, :] = head
            pk[1, k, prow, :] = conduct
            stor[k, rows, :] = storage
            rhs[k, rows, :] = 2.0 * width * (sat_old[k, rows, :] - sq * sq)
            packed = jnp.where(pair_b == k, pltpu.roll(head, 2 * k + 1, 1), packed)
            packed = jnp.where(pair_b == k + 32, pltpu.roll(conduct, 2 * k + 65, 1), packed)
        ypack[1, rows, :] = packed
        return carry

    lax.fori_loop(0, RX // BLOCK, solve_first, 0)

    moves = halo_copies(1)
    for move in moves:
        move.start()
    halo_finish(1, moves)
    lax.fori_loop(0, LAY, sideways, 0)

    def solve_second(r, carry):
        rows = pl.ds(pl.multiple_of(r * BLOCK, BLOCK), BLOCK)
        prow = pl.ds(pl.multiple_of(r * BLOCK + 8, 8), BLOCK)
        head, conduct = pk[0, 0, prow, :], pk[1, 0, prow, :]
        v_prev = flux_prev = q_prev = last = None
        for k in range(LAY):
            target = rhs[k, rows, :] - lat[k, rows, :]
            if k < ROOT:
                target = target - grid[k, rows, :]
            diag = stor[k, rows, :] + gsum[k, rows, :]
            if k < LAY - 1:
                head_n, conduct_n = pk[0, k + 1, prow, :], pk[1, k + 1, prow, :]
                v = 2.0 * (conduct + conduct_n)
                flux = v * (head - head_n + 1.0)
                diag = diag + v
                target = target - flux
            else:
                target = target - 4.0 * conduct
            if k > 0:
                target = target + flux_prev + v_prev * last
                diag = diag + v_prev - v_prev * q_prev
            else:
                target = target + grid[ROOT, rows, :]
            inv = 1.0 / diag
            last = target * inv
            val[k, rows, :] = last
            if k < LAY - 1:
                q_prev = v * inv
                upp[k, rows, :] = q_prev
                head, conduct, v_prev, flux_prev = head_n, conduct_n, v, flux
        numer = denom = jnp.zeros((BLOCK, 128), F32)
        for k in range(LAY - 1, -1, -1):
            if k < LAY - 1:
                last = val[k, rows, :] + upp[k, rows, :] * last
            head = pk[0, k, prow, :] + last
            val[k, rows, :] = head
            if k < ROOT:
                log_s = par_n[k, rows, :] * jnp.log2(
                    par_a[k, rows, :] * jnp.maximum(-head, TINY)
                )
                sat = jnp.exp2(-par_e[k, rows, :] * jnp.log2(1.0 + jnp.exp2(log_s)))
                weight = grid[k, rows, :]
                numer = numer + weight * sat
                denom = denom + weight
        gsum[0, rows, :] = numer / jnp.maximum(denom, TINY)
        return carry

    lax.fori_loop(0, RX // BLOCK, solve_second, 0)
    out_copy = pltpu.make_async_copy(val, p_out, out_sem)
    out_copy.start()

    state = jnp.concatenate([gsum[0, 0:32, :], gsum[0, 32:64, :]], axis=1)
    s_hi = state.astype(BF16)
    left = state - s_hi.astype(F32)
    s_mid = left.astype(BF16)
    s_low = (left - s_mid.astype(F32)).astype(BF16)
    pieces = jnp.concatenate([s_hi, s_mid, s_low], axis=0)
    iota_r1 = lax.broadcasted_iota(I32, (32, 1024), 0)

    def fetch(g, carry):
        got = lax.dot_general(
            pieces, b_mat[g], (((1,), (0,)), ((), ())), preferred_element_type=F32
        )
        got = got[0:32] + got[32:64] + got[64:96]
        line = jnp.sum(jnp.where(iota_r1 == row_of[g], got, 0.0), axis=0, keepdims=True)
        for j in range(8):
            back[g * 8 + j] = line[:, j * 128 : (j + 1) * 128]
        return carry

    lax.fori_loop(0, NX, fetch, 0)

    own_back = pltpu.make_async_copy(back.at[me // 2], mine.at[me], ret_recv)
    own_back.start()

    def reply(i, carry):
        tx, ty = peer(i)
        pltpu.make_async_remote_copy(
            back.at[(tx * NY + ty) // 2], mine.at[me], ret_send, ret_recv,
            device_id=(tx, ty), device_id_type=MESH,
        ).start()
        return carry

    lax.fori_loop(1, PEERS, reply, 0)
    pltpu.make_async_copy(mine, mine, ret_recv).wait()

    parity = lax.rem(me, 2)
    lane1 = lax.broadcasted_iota(I32, (1, 128), 1)

    def take(q, carry):
        even, other = mine[2 * q], mine[2 * q + 1]
        low_half = jnp.where(lane1 < 64, even, pltpu.roll(other, 64, 1))
        high_half = jnp.where(lane1 < 64, pltpu.roll(even, 64, 1), other)
        s_out[q] = jnp.where(parity == 0, low_half, high_half)
        return carry

    lax.fori_loop(0, PEERS // 2, take, 0)

    pltpu.make_async_copy(send.at[0 : PEERS - 1], send.at[0 : PEERS - 1], send_sem).wait()
    pltpu.make_async_copy(mine.at[0 : PEERS - 1], mine.at[0 : PEERS - 1], ret_send).wait()
    out_copy.wait()


def on_device(h_old, soil_type, ks_scale, soil_table, clump_brick, clump_cell, root_fraction,
              transpiration, infiltration):
    del clump_brick
    whole = lambda shape, dtype=F32: pltpu.VMEM(shape, dtype)
    cube = whole((LAY, RX, RY))
    dma = pltpu.SemaphoreType.DMA
    vmem = pl.BlockSpec(memory_space=pltpu.VMEM)
    hbm = pl.BlockSpec(memory_space=pl.ANY)
    scratch = [
        cube, whole((LAY, RX, RY), I32), cube,
        whole((1, SLOTS), I32), whole((ROOT, SLOTS)), whole((1, SLOTS)), whole((1, SLOTS)),
        whole((8, 128)), whole((8, SLOTS)), whole((PEERS, 8, 128)), whole((NX, NY, 8, 128)),
        cube, cube, cube, cube, cube,
        whole((2, LAY, RX + 16, RY)), cube, cube, cube, cube,
        cube, cube, cube, cube, cube,
        whole((FIELDS * 64, 1024), BF16), whole((NX, 256, 1024), BF16),
        whole((NX, 1, 1024), I32), whole((FIELDS * 64, 256)), whole((FIELDS, RX, RY)),
        whole((2, RX, 128)), whole((2, 2, RX, 128)), whole((2, 2, 2, LAY, 8, 128)),
        whole((RX, 128)),
        whole((PEERS // 2, 1, 128)), whole((PEERS, 1, 128)),
        dma((7,)), dma, dma((NX,)), dma((2, 4)), dma((2, 4)), dma, dma, dma,
    ]
    pressure, stress = pl.pallas_call(
        kernel,
        out_shape=(
            jax.ShapeDtypeStruct((LAY, RX, RY), F32),
            jax.ShapeDtypeStruct((PEERS // 2, 1, 128), F32),
        ),
        in_specs=[hbm, hbm, hbm, vmem, hbm, hbm, hbm, hbm],
        out_specs=(hbm, vmem),
        scratch_shapes=scratch,
        compiler_params=pltpu.CompilerParams(
            collective_id=1, has_side_effects=True, vmem_limit_bytes=56 * 1024 * 1024
        ),
        name="step",
    )(
        h_old, soil_type, ks_scale, soil_table, clump_cell.reshape(1, SLOTS), root_fraction,
        transpiration.reshape(1, SLOTS), infiltration.reshape(1, SLOTS),
    )
    return pressure, stress.reshape(SLOTS)


def solution(mesh):
    cells = P(None, "bx", "by")
    slots = P(("bx", "by"))
    return jax.shard_map(
        on_device,
        mesh=mesh,
        in_specs=(cells, cells, cells, P(), slots, slots, P(None, ("bx", "by")), slots, slots),
        out_specs=(cells, slots),
        check_vma=False,
    )
```

profile of v0, /device:TPU:1, one launch (start us, length us, event | category | flops | bytes accessed | tf_op | source)
XLA Modules:
  0.0 64.7 jit_solution(6580982633255192784)
XLA Ops:
  0.6 61.4 %step.1 = (f32[20,64,128]{2,1,0:T(8,128)}, f32[64,1,128]{2,1,0:T(1,128)}) custom-call(f32[20,64,128]{2,1,0:T(8,128)} %h_hbm.1, s32[20,64,128]{2,1,0:T(8,128)} %soil_hbm.1, f32[20,64,128]{2,1,0:T(8,128)} %ks_hbm.1, f32[4,12]{1,0:T(4,128)} %table_ref.1, s32[1,8192]{1,0:T(1,128)} %bitcast.4, f32[14,8192]{1,0:T(8,128)} %root_hbm.1, f32[1,8192]{1,0:T(1,128)} %bitcast.5, ...), custom_call_target="tpu_custom_call" | custom-call | tf_op jit(solution)/shard_map/step/pallas_call | solution.py:442
  62.1 0.0 copy-start
  62.1 2.0 %copy.12 = f32[20,64,128]{2,1,0:T(8,128)} copy(f32[20,64,128]{2,1,0:T(8,128)} %get-tuple-element.8) | data formatting | bytes 1310720
  64.1 0.0 copy-done
  64.1 0.6 copy.13
Async XLA Ops:
  62.1 2.0 %copy-start = (f32[64,1,128]{2,1,0:T(1,128)S(1)}, f32[64,1,128]{2,1,0:T(1,128)}, u32[]{:S(2)}) copy-start(f32[64,1,128]{2,1,0:T(1,128)} %get-tuple-element.5) | copy-start | bytes 98308
where the time goes:
time: 64.9 us; the launch traced here: 64.7 us
  Pallas kernels  61.4 us (95%)
  local copies, waits for them, and re-layouts  2.61 us (4%)
  between operations  0.65 us (1%)
    pallas_call x1, Pallas kernels, on_device(): pl.pallas_call(kernel, out_shape=(jax.ShapeDtypeStruct((LAY, RX, RY), F32...  61.4 us
    unnamed x4, local copies, waits for them, and re-layouts  2.61 us

commit v1 on v0

--- a/solution.py
+++ b/solution.py
@@ -1,4 +1,4 @@
-import functools
+import itertools
 
 import jax
 import jax.numpy as jnp
@@ -19,6 +19,12 @@
 F32, BF16, I32 = jnp.float32, jnp.bfloat16, jnp.int32
 
 
+ORDER = sorted(
+    (o for o in itertools.product(range(4), range(2), range(4), range(4)) if any(o)),
+    key=lambda o: -sum(min(d, 4 - d) for d in (o[0], o[2], o[3])),
+)
+
+
 def closures(head, alpha, shape_n, exponent, ks, width):
     log_s = shape_n * jnp.log2(alpha * jnp.maximum(-head, TINY))
     log_b = jnp.log2(1.0 + jnp.exp2(log_s))
@@ -39,7 +45,7 @@
     pk, sat_old, stor, lat, gsum,
     rinv, low, upp, rhs, val,
     a_mat, b_mat, row_of, acc, grid,
-    ypack, yrecv, xrecv, ycomb,
+    ypack, yrecv, xrecv, ycomb, state_ref,
     back, mine,
     in_sem, send_sem, recv_sem, halo_send, halo_recv, ret_send, ret_recv, out_sem,
 ):
@@ -59,17 +65,19 @@
     for copy in copies:
         copy.start()
 
-    def peer(i):
-        dx, dy = i // NY, lax.rem(i, NY)
-        return lax.rem(bx + dx, NX), lax.rem(by + dy, NY)
+    core = lax.rem(bx, 2)
+    cores = (core, 1 - core)
+    ys = [lax.rem(bx // 2 + d, 4) * 2 for d in range(4)]
+    xs = [lax.rem(by // 4 + d, 4) * 4 for d in range(4)]
+    zs = [lax.rem(by + d, 4) for d in range(4)]
+
+    def peer(offset):
+        y, c, x, z = offset
+        return ys[y] + cores[c], xs[x] + zs[z]
 
     barrier = pltpu.get_barrier_semaphore()
-
-    def greet(i, carry):
-        pl.semaphore_signal(barrier, inc=1, device_id=peer(i), device_id_type=MESH)
-        return carry
-
-    lax.fori_loop(1, PEERS, greet, 0)
+    for offset in ORDER:
+        pl.semaphore_signal(barrier, inc=1, device_id=peer(offset), device_id_type=MESH)
 
     lane8 = lax.broadcasted_iota(I32, (8, 128), 1)
     sub8 = lax.broadcasted_iota(I32, (8, 128), 0)
@@ -92,22 +100,19 @@
         send[2 * q + 1] = jnp.where(first_half, r0, v1)
         return carry
 
-    lax.fori_loop(0, PEERS // 2, pack, 0)
+    lax.fori_loop(0, PEERS // 2, pack, 0, unroll=8)
 
     pl.semaphore_wait(barrier, PEERS - 1)
 
     own = pltpu.make_async_copy(send.at[me], recv.at[bx, by], recv_sem.at[bx])
     own.start()
 
-    def push(i, carry):
-        tx, ty = peer(i)
+    for offset in ORDER:
+        tx, ty = peer(offset)
         pltpu.make_async_remote_copy(
             send.at[tx * NY + ty], recv.at[bx, by], send_sem, recv_sem.at[bx],
             device_id=(tx, ty), device_id_type=MESH,
         ).start()
-        return carry
-
-    lax.fori_loop(1, PEERS, push, 0)
 
     table[...] = jnp.zeros_like(table)
     table[0:4, 0:12] = table_ref[...]
@@ -145,8 +150,8 @@
         left = bx, lax.rem(by + NY - 1, NY)
         right = bx, lax.rem(by + 1, NY)
         moves = (
-            (pk.at[:, :, pl.ds(64, 8), :], xrecv.at[step, 0], down),
-            (pk.at[:, :, pl.ds(8, 8), :], xrecv.at[step, 1], up),
+            (pk.at[:, :, pl.ds(71, 1), :], xrecv.at[step, 0, :, :, pl.ds(0, 1), :], down),
+            (pk.at[:, :, pl.ds(8, 1), :], xrecv.at[step, 1, :, :, pl.ds(0, 1), :], up),
             (ypack.at[step], yrecv.at[step, 0], right),
             (ypack.at[step], yrecv.at[step, 1], left),
         )
@@ -159,51 +164,55 @@
         ]
 
     odd = lax.rem(lane, 2) == 1
+    lane_b = lax.broadcasted_iota(I32, (BLOCK, 128), 1)
+    pair_b = lane_b // 2
 
     def halo_finish(step, moves):
         for move in moves:
             move.wait_recv()
         for move in moves:
             move.wait_send()
-        for k in range(LAY):
-            pk[0, k, 7:8, :] = xrecv[step, 0, 0, k, 7:8, :]
-            pk[0, k, 72:73, :] = xrecv[step, 1, 0, k, 0:1, :]
-            pk[1, k, 7:8, :] = jnp.where(bx == 0, -pk[1, k, 8:9, :], xrecv[step, 0, 1, k, 7:8, :])
-            pk[1, k, 72:73, :] = jnp.where(
-                bx == NX - 1, -pk[1, k, 71:72, :], xrecv[step, 1, 1, k, 0:1, :]
-            )
+        own = ypack[step]
         both = jnp.where(
             odd, pltpu.roll(yrecv[step, 0], 1, 1), pltpu.roll(yrecv[step, 1], 127, 1)
         )
         edge = jnp.logical_or(
             jnp.logical_and(odd, by == 0), jnp.logical_and(jnp.logical_not(odd), by == NY - 1)
         )
-        ycomb[...] = jnp.where(edge, -ypack[step], both)
-
-    at_first, at_last = lane == 0, lane == 127
+        both = jnp.where(edge, -own, both)
+        face = pltpu.roll(own + both, 64, 1)
+        flow = face * (own - both)
+        ycomb[...] = jnp.where(lane < 64, flow, own + both)
+        for k in range(LAY):
+            for side, row, off in ((0, 0, bx == 0), (1, RX - 1, bx == NX - 1)):
+                p_own, k_own = pk[0, k, 8 + row : 9 + row, :], pk[1, k, 8 + row : 9 + row, :]
+                g = k_own + jnp.where(off, -k_own, xrecv[step, side, 1, k, 0:1, :])
+                gsum[k, row : row + 1, :] += g
+                lat[k, row : row + 1, :] += g * (p_own - xrecv[step, side, 0, k, 0:1, :])
+
+    at_first = lane == 0
 
     def sideways(k, carry):
         head, conduct = pk[0, k, 8:72, :], pk[1, k, 8:72, :]
-        comb = ycomb[...]
-        hp = pltpu.roll(comb, 127 - 2 * k, 1)
-        hk = pltpu.roll(comb, 63 - 2 * k, 1)
-        left_p = jnp.where(at_first, hp, pltpu.roll(head, 1, 1))
-        left_k = jnp.where(at_first, hk, pltpu.roll(conduct, 1, 1))
-        right_p = jnp.where(at_last, hp, pltpu.roll(head, 127, 1))
-        right_k = jnp.where(at_last, hk, pltpu.roll(conduct, 127, 1))
-        gl, gr = conduct + left_k, conduct + right_k
-        gu, gd = conduct + pk[1, k, 7:71, :], conduct + pk[1, k, 9:73, :]
-        gsum[k] = (gl + gr) + (gu + gd)
-        lat[k] = (gl * (head - left_p) + gr * (head - right_p)) + (
-            gu * (head - pk[0, k, 7:71, :]) + gd * (head - pk[0, k, 9:73, :])
-        )
+        g = jnp.where(at_first, 0.0, conduct + pltpu.roll(conduct, 1, 1))
+        f = g * (head - pltpu.roll(head, 1, 1))
+        gx = conduct[:-1] + conduct[1:]
+        fx = gx * (head[1:] - head[:-1])
+        zero = jnp.zeros((1, 128), F32)
+        gx0 = jnp.concatenate([zero, gx], axis=0)
+        gx1 = jnp.concatenate([gx, zero], axis=0)
+        fx0 = jnp.concatenate([zero, fx], axis=0)
+        fx1 = jnp.concatenate([fx, zero], axis=0)
+        gsum[k] = (g + pltpu.roll(g, 127, 1)) + (gx0 + gx1)
+        lat[k] = (f - pltpu.roll(f, 127, 1)) + (fx0 - fx1)
         return carry
 
     moves = halo_copies(0)
     for move in moves:
         move.start()
+    lax.fori_loop(0, LAY, sideways, 0)
     halo_finish(0, moves)
-    lax.fori_loop(0, LAY, sideways, 0)
+    ends = jnp.logical_or(lane_b == 0, lane_b == 127)
 
     def factor_first(r, carry):
         rows = pl.ds(pl.multiple_of(r * BLOCK, BLOCK), BLOCK)
@@ -211,8 +220,11 @@
         head, conduct = pk[0, 0, prow, :], pk[1, 0, prow, :]
         v_prev = flux_prev = q_prev = None
         for k in range(LAY):
-            target = -lat[k, rows, :]
-            diag = stor[k, rows, :] + gsum[k, rows, :]
+            comb = ycomb[rows, :]
+            side_f = jnp.where(ends, pltpu.roll(comb, 127 - 2 * k, 1), 0.0)
+            side_g = jnp.where(ends, pltpu.roll(comb, 63 - 2 * k, 1), 0.0)
+            target = -(lat[k, rows, :] + side_f)
+            diag = stor[k, rows, :] + (gsum[k, rows, :] + side_g)
             if k < LAY - 1:
                 head_n, conduct_n = pk[0, k + 1, prow, :], pk[1, k + 1, prow, :]
                 v = 2.0 * (conduct + conduct_n)
@@ -274,9 +286,6 @@
         both = acc[f * 64 : f * 64 + 32, :] + acc[f * 64 + 32 : f * 64 + 64, :]
         grid[f, 0:32, :] = both[:, :128]
         grid[f, 32:64, :] = both[:, 128:]
-    lane_b = lax.broadcasted_iota(I32, (BLOCK, 128), 1)
-    pair_b = lane_b // 2
-
     def solve_first(r, carry):
         rows = pl.ds(pl.multiple_of(r * BLOCK, BLOCK), BLOCK)
         prow = pl.ds(pl.multiple_of(r * BLOCK + 8, 8), BLOCK)
@@ -312,8 +321,8 @@
     moves = halo_copies(1)
     for move in moves:
         move.start()
+    lax.fori_loop(0, LAY, sideways, 0)
     halo_finish(1, moves)
-    lax.fori_loop(0, LAY, sideways, 0)
 
     def solve_second(r, carry):
         rows = pl.ds(pl.multiple_of(r * BLOCK, BLOCK), BLOCK)
@@ -321,10 +330,13 @@
         head, conduct = pk[0, 0, prow, :], pk[1, 0, prow, :]
         v_prev = flux_prev = q_prev = last = None
         for k in range(LAY):
-            target = rhs[k, rows, :] - lat[k, rows, :]
+            comb = ycomb[rows, :]
+            side_f = jnp.where(ends, pltpu.roll(comb, 127 - 2 * k, 1), 0.0)
+            side_g = jnp.where(ends, pltpu.roll(comb, 63 - 2 * k, 1), 0.0)
+            target = rhs[k, rows, :] - (lat[k, rows, :] + side_f)
             if k < ROOT:
                 target = target - grid[k, rows, :]
-            diag = stor[k, rows, :] + gsum[k, rows, :]
+            diag = stor[k, rows, :] + (gsum[k, rows, :] + side_g)
             if k < LAY - 1:
                 head_n, conduct_n = pk[0, k + 1, prow, :], pk[1, k + 1, prow, :]
                 v = 2.0 * (conduct + conduct_n)
@@ -359,14 +371,14 @@
                 weight = grid[k, rows, :]
                 numer = numer + weight * sat
                 denom = denom + weight
-        gsum[0, rows, :] = numer / jnp.maximum(denom, TINY)
+        state_ref[rows, :] = numer / jnp.maximum(denom, TINY)
         return carry
 
     lax.fori_loop(0, RX // BLOCK, solve_second, 0)
     out_copy = pltpu.make_async_copy(val, p_out, out_sem)
     out_copy.start()
 
-    state = jnp.concatenate([gsum[0, 0:32, :], gsum[0, 32:64, :]], axis=1)
+    state = jnp.concatenate([state_ref[0:32, :], state_ref[32:64, :]], axis=1)
     s_hi = state.astype(BF16)
     left = state - s_hi.astype(F32)
     s_mid = left.astype(BF16)
@@ -389,28 +401,18 @@
     own_back = pltpu.make_async_copy(back.at[me // 2], mine.at[me], ret_recv)
     own_back.start()
 
-    def reply(i, carry):
-        tx, ty = peer(i)
+    for offset in ORDER:
+        tx, ty = peer(offset)
         pltpu.make_async_remote_copy(
             back.at[(tx * NY + ty) // 2], mine.at[me], ret_send, ret_recv,
             device_id=(tx, ty), device_id_type=MESH,
         ).start()
-        return carry
-
-    lax.fori_loop(1, PEERS, reply, 0)
     pltpu.make_async_copy(mine, mine, ret_recv).wait()
 
-    parity = lax.rem(me, 2)
-    lane1 = lax.broadcasted_iota(I32, (1, 128), 1)
-
-    def take(q, carry):
-        even, other = mine[2 * q], mine[2 * q + 1]
-        low_half = jnp.where(lane1 < 64, even, pltpu.roll(other, 64, 1))
-        high_half = jnp.where(lane1 < 64, pltpu.roll(even, 64, 1), other)
-        s_out[q] = jnp.where(parity == 0, low_half, high_half)
-        return carry
-
-    lax.fori_loop(0, PEERS // 2, take, 0)
+    even, other = mine[pl.ds(0, 64, 2), 0, :], mine[pl.ds(1, 64, 2), 0, :]
+    low_half = jnp.where(lane < 64, even, pltpu.roll(other, 64, 1))
+    high_half = jnp.where(lane < 64, pltpu.roll(even, 64, 1), other)
+    s_out[...] = jnp.where(lax.rem(me, 2) == 0, low_half, high_half)
 
     pltpu.make_async_copy(send.at[0 : PEERS - 1], send.at[0 : PEERS - 1], send_sem).wait()
     pltpu.make_async_copy(mine.at[0 : PEERS - 1], mine.at[0 : PEERS - 1], ret_send).wait()
@@ -435,7 +437,7 @@
         whole((FIELDS * 64, 1024), BF16), whole((NX, 256, 1024), BF16),
         whole((NX, 1, 1024), I32), whole((FIELDS * 64, 256)), whole((FIELDS, RX, RY)),
         whole((2, RX, 128)), whole((2, 2, RX, 128)), whole((2, 2, 2, LAY, 8, 128)),
-        whole((RX, 128)),
+        whole((RX, 128)), whole((RX, 128)),
         whole((PEERS // 2, 1, 128)), whole((PEERS, 1, 128)),
         dma((7,)), dma, dma((NX,)), dma((2, 4)), dma((2, 4)), dma, dma, dma,
     ]
@@ -443,7 +445,7 @@
         kernel,
         out_shape=(
             jax.ShapeDtypeStruct((LAY, RX, RY), F32),
-            jax.ShapeDtypeStruct((PEERS // 2, 1, 128), F32),
+            jax.ShapeDtypeStruct((PEERS // 2, 128), F32),
         ),
         in_specs=[hbm, hbm, hbm, vmem, hbm, hbm, hbm, hbm],
         out_specs=(hbm, vmem),

time: 64.9 us -> 49.4 us (0.76)
  Pallas kernels: 61.4 us -> 45.9 us
    pallas_call x1, Pallas kernels: 61.4 us -> 45.9 us  [on_device(): pl.pallas_call(kernel, out_shape=(jax.ShapeDtypeStruct((LAY, RX, RY), F32...]
where the time goes in v1:
time: 49.4 us; the launch traced here: 49.2 us
  Pallas kernels  45.9 us (93%)
  local copies, waits for them, and re-layouts  2.61 us (5%)
  between operations  0.65 us (1%)
    pallas_call x1, Pallas kernels, on_device(): pl.pallas_call(kernel, out_shape=(jax.ShapeDtypeStruct((LAY, RX, RY), F32...  45.9 us
    unnamed x4, local copies, waits for them, and re-layouts  2.61 us

profile of v1, /device:TPU:1, one launch (start us, length us, event | category | flops | bytes accessed | tf_op | source)
XLA Modules:
  0.0 49.2 jit_solution(9341317236413839766)
XLA Ops:
  0.6 45.9 %step.1 = (f32[20,64,128]{2,1,0:T(8,128)}, f32[64,128]{1,0:T(8,128)}) custom-call(f32[20,64,128]{2,1,0:T(8,128)} %h_hbm.1, s32[20,64,128]{2,1,0:T(8,128)} %soil_hbm.1, f32[20,64,128]{2,1,0:T(8,128)} %ks_hbm.1, f32[4,12]{1,0:T(4,128)} %table_ref.1, s32[1,8192]{1,0:T(1,128)} %bitcast.4, f32[14,8192]{1,0:T(8,128)} %root_hbm.1, f32[1,8192]{1,0:T(1,128)} %bitcast.5, ...), custom_call_target="tpu_custom_call" | custom-call | tf_op jit(solution)/shard_map/step/pallas_call | solution.py:444
  46.6 0.0 copy-start
  46.6 2.0 %copy.12 = f32[20,64,128]{2,1,0:T(8,128)} copy(f32[20,64,128]{2,1,0:T(8,128)} %get-tuple-element.8) | data formatting | bytes 1310720
  48.6 0.0 copy-done
  48.6 0.6 %copy.13 = f32[8192]{0:T(1024)} copy(f32[8192]{0:T(1024)S(1)} %bitcast.7) | data formatting | bytes 65536
Async XLA Ops:
  46.6 2.0 %copy-start = (f32[64,128]{1,0:T(8,128)S(1)}, f32[64,128]{1,0:T(8,128)}, u32[]{:S(2)}) copy-start(f32[64,128]{1,0:T(8,128)} %get-tuple-element.5) | copy-start | bytes 98308

commit v2 on v1

--- a/solution.py
+++ b/solution.py
@@ -19,10 +19,33 @@
 F32, BF16, I32 = jnp.float32, jnp.bfloat16, jnp.int32
 
 
-ORDER = sorted(
-    (o for o in itertools.product(range(4), range(2), range(4), range(4)) if any(o)),
-    key=lambda o: -sum(min(d, 4 - d) for d in (o[0], o[2], o[3])),
+def ring(d):
+    return min(d, 4 - d)
+
+
+PAIRS = sorted(
+    itertools.product(range(4), range(2), range(4), range(2)),
+    key=lambda o: (ring(o[0]) + ring(o[2]) + o[3], o[1], ring(o[0])),
 )
+GROUPS, PER = 8, 8
+WAVES = (0, 1, 2, 3, 4, 5, 6, 7)
+PLACE = {
+    pair: wave * PER + i
+    for wave, group in enumerate(WAVES)
+    for i, pair in enumerate(PAIRS[group * PER : group * PER + PER])
+}
+OWN = PLACE[0, 0, 0, 0]
+TARGETS = [
+    (pair, b)
+    for group in WAVES
+    for pair in reversed(PAIRS[group * PER : group * PER + PER])
+    for b in (1, 0)
+    if any(pair) or b
+]
+
+
+def seen_back(pair):
+    return PLACE[-pair[0] % 4, pair[1], -pair[2] % 4, pair[3]]
 
 
 def closures(head, alpha, shape_n, exponent, ks, width):
@@ -44,7 +67,7 @@
     par_a, par_n, par_e, par_k, par_w,
     pk, sat_old, stor, lat, gsum,
     rinv, low, upp, rhs, val,
-    a_mat, b_mat, row_of, acc, grid,
+    b_mat, row_of, acc, grid,
     ypack, yrecv, xrecv, ycomb, state_ref,
     back, mine,
     in_sem, send_sem, recv_sem, halo_send, halo_recv, ret_send, ret_recv, out_sem,
@@ -69,15 +92,18 @@
     cores = (core, 1 - core)
     ys = [lax.rem(bx // 2 + d, 4) * 2 for d in range(4)]
     xs = [lax.rem(by // 4 + d, 4) * 4 for d in range(4)]
-    zs = [lax.rem(by + d, 4) for d in range(4)]
-
-    def peer(offset):
-        y, c, x, z = offset
-        return ys[y] + cores[c], xs[x] + zs[z]
+    half = lax.rem(by, 2)
+    halves = (half, 1 - half)
+    upper = lax.rem(by, 4) - half
+    zs = (upper, 2 - upper)
+
+    def peer(target):
+        (y, c, x, z), b = target
+        return ys[y] + cores[c], xs[x] + zs[z] + halves[b]
 
     barrier = pltpu.get_barrier_semaphore()
-    for offset in ORDER:
-        pl.semaphore_signal(barrier, inc=1, device_id=peer(offset), device_id_type=MESH)
+    for target in TARGETS:
+        pl.semaphore_signal(barrier, inc=1, device_id=peer(target), device_id_type=MESH)
 
     lane8 = lax.broadcasted_iota(I32, (8, 128), 1)
     sub8 = lax.broadcasted_iota(I32, (8, 128), 0)
@@ -101,18 +127,6 @@
         return carry
 
     lax.fori_loop(0, PEERS // 2, pack, 0, unroll=8)
-
-    pl.semaphore_wait(barrier, PEERS - 1)
-
-    own = pltpu.make_async_copy(send.at[me], recv.at[bx, by], recv_sem.at[bx])
-    own.start()
-
-    for offset in ORDER:
-        tx, ty = peer(offset)
-        pltpu.make_async_remote_copy(
-            send.at[tx * NY + ty], recv.at[bx, by], send_sem, recv_sem.at[bx],
-            device_id=(tx, ty), device_id_type=MESH,
-        ).start()
 
     table[...] = jnp.zeros_like(table)
     table[0:4, 0:12] = table_ref[...]
@@ -143,6 +157,8 @@
         return packed
 
     ypack[0] = lax.fori_loop(0, LAY, first, jnp.zeros((RX, 128), F32))
+
+    pl.semaphore_wait(barrier, PEERS - 1)
 
     def halo_copies(step):
         up = lax.rem(bx + NX - 1, NX), by
@@ -210,7 +226,58 @@
     moves = halo_copies(0)
     for move in moves:
         move.start()
+
+    pltpu.make_async_copy(send.at[me], recv.at[OWN, half], recv_sem.at[OWN // PER]).start()
+    for target in TARGETS:
+        tx, ty = peer(target)
+        spot = seen_back(target[0])
+        pltpu.make_async_remote_copy(
+            send.at[tx * NY + ty], recv.at[spot, half], send_sem, recv_sem.at[spot // PER],
+            device_id=(tx, ty), device_id_type=MESH,
+        ).start()
+
     lax.fori_loop(0, LAY, sideways, 0)
+    iota_c = lax.broadcasted_iota(I32, (256, 128), 0)
+    iota_r = lax.broadcasted_iota(I32, (32, 128), 0)
+    acc[...] = jnp.zeros_like(acc)
+
+    def spread_tile(g, j):
+        m0, m1 = recv[g * PER + j, 0], recv[g * PER + j, 1]
+        v0 = jnp.where(first_half, m0, pltpu.roll(m1, 64, 1))
+        v1 = jnp.where(first_half, pltpu.roll(m0, 64, 1), m1)
+        at = slice(j * 128, (j + 1) * 128)
+        spot = v1[7:8, :].astype(I32)
+        brow = spot >> 7
+        col = (spot & 127) + ((brow >> 5) << 7)
+        brow = brow & 31
+        row_of[g, :, at] = brow
+        b_mat[g, :, at] = jnp.where(iota_c == col, 1.0, 0.0).astype(BF16)
+        hit = iota_r == brow
+        spread = lambda line: jnp.where(hit, line, 0.0).astype(BF16)
+        h0 = v0.astype(BF16).astype(F32)
+        h1 = v1.astype(BF16).astype(F32)
+        pieces = []
+        for f in range(FIELDS):
+            high, whole = (h0, v0) if f < 8 else (h1, v1)
+            row = slice(f % 8, f % 8 + 1)
+            pieces.append(spread(high[row]))
+            pieces.append(spread((whole - high)[row]))
+        return jnp.concatenate(pieces, axis=0)
+
+    def place(g, carry):
+        part_of = recv.at[pl.ds(g * PER, PER)]
+        pltpu.make_async_copy(part_of, part_of, recv_sem.at[g]).wait()
+        for part in range(PER // 2):
+            blocks = []
+            for j in range(part * 2, part * 2 + 2):
+                blocks.append(spread_tile(g, j))
+            a_val = jnp.concatenate(blocks, axis=1) if len(blocks) > 1 else blocks[0]
+            acc[...] += lax.dot_general(
+                a_val, b_mat[g, :, part * 256 : part * 256 + 256], (((1,), (1,)), ((), ())),
+                preferred_element_type=F32,
+            )
+        return carry
+
     halo_finish(0, moves)
     ends = jnp.logical_or(lane_b == 0, lane_b == 127)
 
@@ -248,40 +315,8 @@
         return carry
 
     lax.fori_loop(0, RX // BLOCK, factor_first, 0)
-
-    iota_c = lax.broadcasted_iota(I32, (256, 128), 0)
-    iota_r = lax.broadcasted_iota(I32, (32, 128), 0)
-    acc[...] = jnp.zeros_like(acc)
-
-    def place(g, carry):
-        sx = lax.rem(bx + g, NX)
-        pltpu.make_async_copy(recv.at[sx], recv.at[sx], recv_sem.at[sx]).wait()
-        for j in range(NY // 2):
-            m0, m1 = recv[sx, 2 * j], recv[sx, 2 * j + 1]
-            v0 = jnp.where(first_half, m0, pltpu.roll(m1, 64, 1))
-            v1 = jnp.where(first_half, pltpu.roll(m0, 64, 1), m1)
-            at = slice(j * 128, (j + 1) * 128)
-            spot = v1[7:8, :].astype(I32)
-            brow = spot >> 7
-            col = (spot & 127) + ((brow >> 5) << 7)
-            brow = brow & 31
-            row_of[sx, :, at] = brow
-            b_mat[sx, :, at] = jnp.where(iota_c == col, 1.0, 0.0).astype(BF16)
-            hit = iota_r == brow
-            h0 = v0.astype(BF16).astype(F32)
-            h1 = v1.astype(BF16).astype(F32)
-            l0, l1 = v0 - h0, v1 - h1
-            for f in range(FIELDS):
-                hi = h0[f : f + 1] if f < 8 else h1[f - 8 : f - 7]
-                lo = l0[f : f + 1] if f < 8 else l1[f - 8 : f - 7]
-                a_mat[f * 64 : f * 64 + 32, at] = jnp.where(hit, hi, 0.0).astype(BF16)
-                a_mat[f * 64 + 32 : f * 64 + 64, at] = jnp.where(hit, lo, 0.0).astype(BF16)
-        acc[...] += lax.dot_general(
-            a_mat[...], b_mat[sx], (((1,), (1,)), ((), ())), preferred_element_type=F32
-        )
-        return carry
-
-    lax.fori_loop(0, NX, place, 0)
+    lax.fori_loop(0, GROUPS, place, 0)
+
     for f in range(FIELDS):
         both = acc[f * 64 : f * 64 + 32, :] + acc[f * 64 + 32 : f * 64 + 64, :]
         grid[f, 0:32, :] = both[:, :128]
@@ -386,27 +421,22 @@
     pieces = jnp.concatenate([s_hi, s_mid, s_low], axis=0)
     iota_r1 = lax.broadcasted_iota(I32, (32, 1024), 0)
 
-    def fetch(g, carry):
+    for g in sorted(range(GROUPS), key=lambda w: -WAVES[w]):
         got = lax.dot_general(
             pieces, b_mat[g], (((1,), (0,)), ((), ())), preferred_element_type=F32
         )
         got = got[0:32] + got[32:64] + got[64:96]
         line = jnp.sum(jnp.where(iota_r1 == row_of[g], got, 0.0), axis=0, keepdims=True)
-        for j in range(8):
-            back[g * 8 + j] = line[:, j * 128 : (j + 1) * 128]
-        return carry
-
-    lax.fori_loop(0, NX, fetch, 0)
-
-    own_back = pltpu.make_async_copy(back.at[me // 2], mine.at[me], ret_recv)
-    own_back.start()
-
-    for offset in ORDER:
-        tx, ty = peer(offset)
-        pltpu.make_async_remote_copy(
-            back.at[(tx * NY + ty) // 2], mine.at[me], ret_send, ret_recv,
-            device_id=(tx, ty), device_id_type=MESH,
-        ).start()
+        for j in range(PER):
+            back[g * PER + j] = line[:, j * 128 : (j + 1) * 128]
+        for target in TARGETS:
+            spot = PLACE[target[0]]
+            if spot // PER == g:
+                pltpu.make_async_remote_copy(
+                    back.at[spot], mine.at[me], ret_send, ret_recv,
+                    device_id=peer(target), device_id_type=MESH,
+                ).start()
+    pltpu.make_async_copy(back.at[OWN], mine.at[me], ret_recv).start()
     pltpu.make_async_copy(mine, mine, ret_recv).wait()
 
     even, other = mine[pl.ds(0, 64, 2), 0, :], mine[pl.ds(1, 64, 2), 0, :]
@@ -430,16 +460,16 @@
     scratch = [
         cube, whole((LAY, RX, RY), I32), cube,
         whole((1, SLOTS), I32), whole((ROOT, SLOTS)), whole((1, SLOTS)), whole((1, SLOTS)),
-        whole((8, 128)), whole((8, SLOTS)), whole((PEERS, 8, 128)), whole((NX, NY, 8, 128)),
+        whole((8, 128)), whole((8, SLOTS)), whole((PEERS, 8, 128)), whole((PEERS // 2, 2, 8, 128)),
         cube, cube, cube, cube, cube,
         whole((2, LAY, RX + 16, RY)), cube, cube, cube, cube,
         cube, cube, cube, cube, cube,
-        whole((FIELDS * 64, 1024), BF16), whole((NX, 256, 1024), BF16),
-        whole((NX, 1, 1024), I32), whole((FIELDS * 64, 256)), whole((FIELDS, RX, RY)),
+        whole((GROUPS, 256, 1024), BF16),
+        whole((GROUPS, 1, 1024), I32), whole((FIELDS * 64, 256)), whole((FIELDS, RX, RY)),
         whole((2, RX, 128)), whole((2, 2, RX, 128)), whole((2, 2, 2, LAY, 8, 128)),
         whole((RX, 128)), whole((RX, 128)),
         whole((PEERS // 2, 1, 128)), whole((PEERS, 1, 128)),
-        dma((7,)), dma, dma((NX,)), dma((2, 4)), dma((2, 4)), dma, dma, dma,
+        dma((7,)), dma, dma((GROUPS,)), dma((2, 4)), dma((2, 4)), dma, dma, dma,
     ]
     pressure, stress = pl.pallas_call(
         kernel,

time: 49.4 us -> 44.8 us (0.907)
  Pallas kernels: 45.9 us -> 41.4 us
    pallas_call x1, Pallas kernels: 45.9 us -> 41.4 us  [on_device(): pl.pallas_call(kernel, out_shape=(jax.ShapeDtypeStruct((LAY, RX, RY), F32...]
where the time goes in v2:
time: 44.8 us; the launch traced here: 44.6 us
  Pallas kernels  41.4 us (92%)
  local copies, waits for them, and re-layouts  2.61 us (6%)
  between operations  0.65 us (1%)
    pallas_call x1, Pallas kernels, on_device(): pl.pallas_call(kernel, out_shape=(jax.ShapeDtypeStruct((LAY, RX, RY), F32...  41.4 us
    unnamed x4, local copies, waits for them, and re-layouts  2.61 us

profile of v2, /device:TPU:1, one launch (start us, length us, event | category | flops | bytes accessed | tf_op | source)
XLA Modules:
  0.0 44.6 jit_solution(15259253992011011110)
XLA Ops:
  0.6 41.4 %step.1 = (f32[20,64,128]{2,1,0:T(8,128)}, f32[64,128]{1,0:T(8,128)}) custom-call(f32[20,64,128]{2,1,0:T(8,128)} %h_hbm.1, s32[20,64,128]{2,1,0:T(8,128)} %soil_hbm.1, f32[20,64,128]{2,1,0:T(8,128)} %ks_hbm.1, f32[4,12]{1,0:T(4,128)} %table_ref.1, s32[1,8192]{1,0:T(1,128)} %bitcast.4, f32[14,8192]{1,0:T(8,128)} %root_hbm.1, f32[1,8192]{1,0:T(1,128)} %bitcast.5, ...), custom_call_target="tpu_custom_call" | custom-call | tf_op jit(solution)/shard_map/step/pallas_call | solution.py:474
  42.0 0.0 copy-start
  42.0 2.0 %copy.12 = f32[20,64,128]{2,1,0:T(8,128)} copy(f32[20,64,128]{2,1,0:T(8,128)} %get-tuple-element.8) | data formatting | bytes 1310720
  44.0 0.0 copy-done
  44.0 0.6 %copy.13 = f32[8192]{0:T(1024)} copy(f32[8192]{0:T(1024)S(1)} %bitcast.7) | data formatting | bytes 65536
Async XLA Ops:
  42.0 2.0 %copy-start = (f32[64,128]{1,0:T(8,128)S(1)}, f32[64,128]{1,0:T(8,128)}, u32[]{:S(2)}) copy-start(f32[64,128]{1,0:T(8,128)} %get-tuple-element.5) | copy-start | bytes 98308

commit v3 on v2

--- a/solution.py
+++ b/solution.py
@@ -167,7 +167,7 @@
         right = bx, lax.rem(by + 1, NY)
         moves = (
             (pk.at[:, :, pl.ds(71, 1), :], xrecv.at[step, 0, :, :, pl.ds(0, 1), :], down),
-            (pk.at[:, :, pl.ds(8, 1), :], xrecv.at[step, 1, :, :, pl.ds(0, 1), :], up),
+            (pk.at[:, :, pl.ds(8, 1), :], xrecv.at[step, 1, :, :, pl.ds(7, 1), :], up),
             (ypack.at[step], yrecv.at[step, 0], right),
             (ypack.at[step], yrecv.at[step, 1], left),
         )
@@ -199,12 +199,16 @@
         face = pltpu.roll(own + both, 64, 1)
         flow = face * (own - both)
         ycomb[...] = jnp.where(lane < 64, flow, own + both)
-        for k in range(LAY):
-            for side, row, off in ((0, 0, bx == 0), (1, RX - 1, bx == NX - 1)):
-                p_own, k_own = pk[0, k, 8 + row : 9 + row, :], pk[1, k, 8 + row : 9 + row, :]
-                g = k_own + jnp.where(off, -k_own, xrecv[step, side, 1, k, 0:1, :])
-                gsum[k, row : row + 1, :] += g
-                lat[k, row : row + 1, :] += g * (p_own - xrecv[step, side, 0, k, 0:1, :])
+        for side, row, off in ((0, 0, bx == 0), (1, 7, bx == NX - 1)):
+            tile = pl.ds(side * (RX - 8), 8)
+            owned = pl.ds(side * (RX - 8) + 8, 8)
+            here = sub8 == row
+            for k in range(LAY):
+                k_own = pk[1, k, owned, :]
+                g = k_own + jnp.where(off, -k_own, xrecv[step, side, 1, k])
+                f = g * (pk[0, k, owned, :] - xrecv[step, side, 0, k])
+                gsum[k, tile, :] += jnp.where(here, g, 0.0)
+                lat[k, tile, :] += jnp.where(here, f, 0.0)
 
     at_first = lane == 0
 
@@ -449,6 +453,26 @@
     out_copy.wait()
 
 
+def deliver(p_in, s_in, p_out, s_out, held, line, sem_in, sem_out):
+    steps = [
+        (p_in.at[pl.ds(k, 4)], held.at[pl.ds(k, 4)], p_out.at[pl.ds(k, 4)]) for k in range(0, LAY, 4)
+    ]
+    steps.append((s_in, line, s_out))
+    reads = [
+        pltpu.make_async_copy(a, b, sem_in.at[i]) for i, (a, b, _) in enumerate(steps)
+    ]
+    writes = [
+        pltpu.make_async_copy(b, c, sem_out.at[i]) for i, (_, b, c) in enumerate(steps)
+    ]
+    for read in reads:
+        read.start()
+    for read, write in zip(reads, writes):
+        read.wait()
+        write.start()
+    for write in writes:
+        write.wait()
+
+
 def on_device(h_old, soil_type, ks_scale, soil_table, clump_brick, clump_cell, root_fraction,
               transpiration, infiltration):
     del clump_brick
@@ -488,6 +512,17 @@
         h_old, soil_type, ks_scale, soil_table, clump_cell.reshape(1, SLOTS), root_fraction,
         transpiration.reshape(1, SLOTS), infiltration.reshape(1, SLOTS),
     )
+    pressure, stress = pl.pallas_call(
+        deliver,
+        out_shape=(
+            jax.ShapeDtypeStruct((LAY, RX, RY), F32),
+            jax.ShapeDtypeStruct((PEERS // 2, 128), F32),
+        ),
+        in_specs=[hbm, hbm],
+        out_specs=(hbm, hbm),
+        scratch_shapes=[cube, whole((PEERS // 2, 128)), dma((6,)), dma((6,))],
+        name="deliver",
+    )(pressure, stress)
     return pressure, stress.reshape(SLOTS)
 
 

time: 44.8 us -> 44.2 us (0.987)
  local copies, waits for them, and re-layouts: 2.61 us -> 0 us
  Pallas kernels: 41.4 us -> 43.4 us
    unnamed x4 -> x0, local copies, waits for them, and re-layouts: 2.61 us -> none
    pallas_call x0 -> x1, Pallas kernels: none -> 1.93 us  [on_device(): pl.pallas_call(deliver, out_shape=(jax.ShapeDtypeStruct((LAY, RX, RY), F3...]
where the time goes in v3:
time: 44.2 us; the launch traced here: 44.1 us
  Pallas kernels  43.4 us (98%)
  between operations  0.64 us (1%)
    pallas_call x1, Pallas kernels, on_device(): pl.pallas_call(kernel, out_shape=(jax.ShapeDtypeStruct((LAY, RX, RY), F32...  41.5 us
    pallas_call x1, Pallas kernels, on_device(): pl.pallas_call(deliver, out_shape=(jax.ShapeDtypeStruct((LAY, RX, RY), F3...  1.93 us

profile of v3, /device:TPU:1, one launch (start us, length us, event | category | flops | bytes accessed | tf_op | source)
XLA Modules:
  0.0 44.1 jit_solution(13901863625067177710)
XLA Ops:
  0.6 41.5 %step.1 = (f32[20,64,128]{2,1,0:T(8,128)}, f32[64,128]{1,0:T(8,128)}) custom-call(f32[20,64,128]{2,1,0:T(8,128)} %h_hbm.1, s32[20,64,128]{2,1,0:T(8,128)} %soil_hbm.1, f32[20,64,128]{2,1,0:T(8,128)} %ks_hbm.1, f32[4,12]{1,0:T(4,128)} %table_ref.1, s32[1,8192]{1,0:T(1,128)} %bitcast.4, f32[14,8192]{1,0:T(8,128)} %root_hbm.1, f32[1,8192]{1,0:T(1,128)} %bitcast.5, ...), custom_call_target="tpu_custom_call" | custom-call | tf_op jit(solution)/shard_map/step/pallas_call | solution.py:498
  42.1 1.9 %deliver.1 = (f32[20,64,128]{2,1,0:T(8,128)}, f32[64,128]{1,0:T(8,128)}) custom-call(f32[20,64,128]{2,1,0:T(8,128)} %get-tuple-element.6.p_in, f32[64,128]{1,0:T(8,128)} %get-tuple-element.7.s_in), custom_call_target="tpu_custom_call" | custom-call | tf_op jit(solution)/shard_map/deliver/pallas_call | solution.py:515

commit v4 on v3

--- a/solution.py
+++ b/solution.py
@@ -17,6 +17,7 @@
 BLOCK = 16
 TINY = 1e-30
 F32, BF16, I32 = jnp.float32, jnp.bfloat16, jnp.int32
+F8 = jnp.float8_e4m3fn
 
 
 def ring(d):
@@ -258,27 +259,32 @@
         b_mat[g, :, at] = jnp.where(iota_c == col, 1.0, 0.0).astype(BF16)
         hit = iota_r == brow
         spread = lambda line: jnp.where(hit, line, 0.0).astype(BF16)
+        fine = lambda line: jnp.where(hit, line, 0.0).astype(F8)
         h0 = v0.astype(BF16).astype(F32)
         h1 = v1.astype(BF16).astype(F32)
-        pieces = []
+        high, low_part = [], []
         for f in range(FIELDS):
-            high, whole = (h0, v0) if f < 8 else (h1, v1)
+            top, whole_v = (h0, v0) if f < 8 else (h1, v1)
             row = slice(f % 8, f % 8 + 1)
-            pieces.append(spread(high[row]))
-            pieces.append(spread((whole - high)[row]))
-        return jnp.concatenate(pieces, axis=0)
+            high.append(spread(top[row]))
+            if f < ROOT:
+                low_part.append(fine(((whole_v - top) * 32768.0)[row]))
+        high.append(spread((v1 - h1)[6:7]))
+        cols = jnp.where(iota_c == col, 1.0, 0.0).astype(F8)
+        return jnp.concatenate(high, axis=0), jnp.concatenate(low_part, axis=0), cols
 
     def place(g, carry):
         part_of = recv.at[pl.ds(g * PER, PER)]
         pltpu.make_async_copy(part_of, part_of, recv_sem.at[g]).wait()
         for part in range(PER // 2):
-            blocks = []
-            for j in range(part * 2, part * 2 + 2):
-                blocks.append(spread_tile(g, j))
-            a_val = jnp.concatenate(blocks, axis=1) if len(blocks) > 1 else blocks[0]
-            acc[...] += lax.dot_general(
-                a_val, b_mat[g, :, part * 256 : part * 256 + 256], (((1,), (1,)), ((), ())),
-                preferred_element_type=F32,
+            blocks = [spread_tile(g, j) for j in range(part * 2, part * 2 + 2)]
+            high, low_part, cols = (jnp.concatenate(b, axis=1) for b in zip(*blocks))
+            dims = (((1,), (1,)), ((), ()))
+            acc[0 : FIELDS * 32 + 32] += lax.dot_general(
+                high, b_mat[g, :, part * 256 : part * 256 + 256], dims, preferred_element_type=F32
+            )
+            acc[FIELDS * 32 + 32 : FIELDS * 64] += lax.dot_general(
+                low_part, cols, dims, preferred_element_type=F32
             )
         return carry
 
@@ -322,7 +328,11 @@
     lax.fori_loop(0, GROUPS, place, 0)
 
     for f in range(FIELDS):
-        both = acc[f * 64 : f * 64 + 32, :] + acc[f * 64 + 32 : f * 64 + 64, :]
+        if f < ROOT:
+            low_acc = acc[(FIELDS + 1 + f) * 32 : (FIELDS + 2 + f) * 32, :] * (1.0 / 32768.0)
+        else:
+            low_acc = acc[FIELDS * 32 : FIELDS * 32 + 32, :]
+        both = acc[f * 32 : f * 32 + 32, :] + low_acc
         grid[f, 0:32, :] = both[:, :128]
         grid[f, 32:64, :] = both[:, 128:]
     def solve_first(r, carry):

time: 44.2 us -> 43.2 us (0.977)
  Pallas kernels: 43.4 us -> 42.4 us
    pallas_call x1, Pallas kernels: 41.5 us -> 40.4 us  [on_device(): pl.pallas_call(kernel, out_shape=(jax.ShapeDtypeStruct((LAY, RX, RY), F32...]
where the time goes in v4:
time: 43.2 us; the launch traced here: 43 us
  Pallas kernels  42.4 us (98%)
  between operations  0.64 us (1%)
    pallas_call x1, Pallas kernels, on_device(): pl.pallas_call(kernel, out_shape=(jax.ShapeDtypeStruct((LAY, RX, RY), F32...  40.4 us
    pallas_call x1, Pallas kernels, on_device(): pl.pallas_call(deliver, out_shape=(jax.ShapeDtypeStruct((LAY, RX, RY), F3...  1.93 us

profile of v4, /device:TPU:1, one launch (start us, length us, event | category | flops | bytes accessed | tf_op | source)
XLA Modules:
  0.0 43.0 jit_solution(13822484039295218238)
XLA Ops:
  0.6 40.4 %step.1 = (f32[20,64,128]{2,1,0:T(8,128)}, f32[64,128]{1,0:T(8,128)}) custom-call(f32[20,64,128]{2,1,0:T(8,128)} %h_hbm.1, s32[20,64,128]{2,1,0:T(8,128)} %soil_hbm.1, f32[20,64,128]{2,1,0:T(8,128)} %ks_hbm.1, f32[4,12]{1,0:T(4,128)} %table_ref.1, s32[1,8192]{1,0:T(1,128)} %bitcast.4, f32[14,8192]{1,0:T(8,128)} %root_hbm.1, f32[1,8192]{1,0:T(1,128)} %bitcast.5, ...), custom_call_target="tpu_custom_call" | custom-call | tf_op jit(solution)/shard_map/step/pallas_call | solution.py:508
  41.1 1.9 %deliver.1 = (f32[20,64,128]{2,1,0:T(8,128)}, f32[64,128]{1,0:T(8,128)}) custom-call(f32[20,64,128]{2,1,0:T(8,128)} %get-tuple-element.6.p_in, f32[64,128]{1,0:T(8,128)} %get-tuple-element.7.s_in), custom_call_target="tpu_custom_call" | custom-call | tf_op jit(solution)/shard_map/deliver/pallas_call | solution.py:525

commit v5 on v4

--- a/solution.py
+++ b/solution.py
@@ -14,7 +14,7 @@
 RX, RY = 64, 128
 SLOTS = RX * RY
 FIELDS = ROOT + 1
-BLOCK = 16
+BLOCK = 32
 TINY = 1e-30
 F32, BF16, I32 = jnp.float32, jnp.bfloat16, jnp.int32
 F8 = jnp.float8_e4m3fn
@@ -429,17 +429,15 @@
 
     state = jnp.concatenate([state_ref[0:32, :], state_ref[32:64, :]], axis=1)
     s_hi = state.astype(BF16)
-    left = state - s_hi.astype(F32)
-    s_mid = left.astype(BF16)
-    s_low = (left - s_mid.astype(F32)).astype(BF16)
-    pieces = jnp.concatenate([s_hi, s_mid, s_low], axis=0)
+    s_low = (state - s_hi.astype(F32)).astype(BF16)
+    pieces = jnp.concatenate([s_hi, s_low], axis=0)
     iota_r1 = lax.broadcasted_iota(I32, (32, 1024), 0)
 
     for g in sorted(range(GROUPS), key=lambda w: -WAVES[w]):
         got = lax.dot_general(
             pieces, b_mat[g], (((1,), (0,)), ((), ())), preferred_element_type=F32
         )
-        got = got[0:32] + got[32:64] + got[64:96]
+        got = got[0:32] + got[32:64]
         line = jnp.sum(jnp.where(iota_r1 == row_of[g], got, 0.0), axis=0, keepdims=True)
         for j in range(PER):
             back[g * PER + j] = line[:, j * 128 : (j + 1) * 128]

time: 43.2 us -> 42.3 us (0.979)
  Pallas kernels: 42.4 us -> 41.5 us
    pallas_call x1, Pallas kernels: 40.4 us -> 39.6 us  [on_device(): pl.pallas_call(kernel, out_shape=(jax.ShapeDtypeStruct((LAY, RX, RY), F32...]
where the time goes in v5:
time: 42.3 us; the launch traced here: 42.2 us
  Pallas kernels  41.5 us (98%)
  between operations  0.64 us (2%)
    pallas_call x1, Pallas kernels, on_device(): pl.pallas_call(kernel, out_shape=(jax.ShapeDtypeStruct((LAY, RX, RY), F32...  39.6 us
    pallas_call x1, Pallas kernels, on_device(): pl.pallas_call(deliver, out_shape=(jax.ShapeDtypeStruct((LAY, RX, RY), F3...  1.93 us

profile of v5, /device:TPU:1, one launch (start us, length us, event | category | flops | bytes accessed | tf_op | source)
XLA Modules:
  0.0 42.2 jit_solution(15777787749946419362)
XLA Ops:
  0.6 39.6 %step.1 = (f32[20,64,128]{2,1,0:T(8,128)}, f32[64,128]{1,0:T(8,128)}) custom-call(f32[20,64,128]{2,1,0:T(8,128)} %h_hbm.1, s32[20,64,128]{2,1,0:T(8,128)} %soil_hbm.1, f32[20,64,128]{2,1,0:T(8,128)} %ks_hbm.1, f32[4,12]{1,0:T(4,128)} %table_ref.1, s32[1,8192]{1,0:T(1,128)} %bitcast.4, f32[14,8192]{1,0:T(8,128)} %root_hbm.1, f32[1,8192]{1,0:T(1,128)} %bitcast.5, ...), custom_call_target="tpu_custom_call" | custom-call | tf_op jit(solution)/shard_map/step/pallas_call | solution.py:506
  40.2 1.9 %deliver.1 = (f32[20,64,128]{2,1,0:T(8,128)}, f32[64,128]{1,0:T(8,128)}) custom-call(f32[20,64,128]{2,1,0:T(8,128)} %get-tuple-element.6.p_in, f32[64,128]{1,0:T(8,128)} %get-tuple-element.7.s_in), custom_call_target="tpu_custom_call" | custom-call | tf_op jit(solution)/shard_map/deliver/pallas_call | solution.py:523
